TPU v7x, 32 devices: a whole 2x2x4 slice. The times are simulated.
32 devices in a mesh: layer: 4 (over x, core), feat: 8 (over z, y).
Axes of the slice: x: 2, y: 2, z: 4, core: 2. Of those that a mesh axis runs over, the one named last changes fastest.
Arguments:
- layer_acts: bfloat16 [4, 512, 576], P('layer', 'feat'), may hold values from -6 to 6
- enc_weight: bfloat16 [4, 576, 16384], P('layer', None, 'feat'), may hold values from -6 to 6
- dec_weight: bfloat16 [4, 16384, 576], P('layer', 'feat'), may hold values from -6 to 6
- enc_bias: float32 [16384], P('feat'), may hold values from -4 to 4
- dec_bias: float32 [4, 576], P('layer'), may hold values from -4 to 4
Outputs:
- enc_step: bfloat16 [4, 576, 16384], P('layer', None, 'feat')
- dec_step: bfloat16 [4, 16384, 576], P('layer', 'feat')
All inputs are finite; a program needn't handle non-finite values.
Results may differ from a plain program's by a relative error of at most 0.012.
Values may be sent and summed in bfloat16 or wider, within the bound.
A program may use at most 64 MiB of HBM per device.

v0:
```python
import jax
import jax.numpy as jnp
from jax import lax
from jax.sharding import PartitionSpec as P

LEARN_RATE = 4.0


def contract_rows(left, right):
    return lax.dot_general(
        left, right, (((0,), (0,)), ((), ())), preferred_element_type=jnp.float32
    )


def body(layer_acts, enc_weight, dec_weight, enc_bias, dec_bias):
    tok_local = layer_acts[0]
    enc_local = enc_weight[0]
    dec_local = dec_weight[0]
    model_width = enc_local.shape[0]
    slab_width = enc_local.shape[1]
    enc_scale = (layer_acts.shape[0] * lax.axis_size("layer") * model_width) ** (-0.5)
    dec_scale = (slab_width * lax.axis_size("feat")) ** (-0.5)
    whole_tokens = lax.all_gather(tok_local, "feat", axis=0, tiled=True)
    partial_value = jnp.dot(whole_tokens, enc_local, preferred_element_type=jnp.float32)
    preact = enc_scale * lax.psum(partial_value, "layer") + enc_bias
    active_b = jnp.maximum(preact, 0.0).astype(jnp.bfloat16)
    recon = lax.psum_scatter(
        dec_scale * jnp.dot(active_b, dec_local, preferred_element_type=jnp.float32),
        "feat",
        scatter_dimension=0,
        tiled=True,
    )
    error_b = (recon + dec_bias[0] - tok_local.astype(jnp.float32)).astype(jnp.bfloat16)
    whole_errors = lax.all_gather(error_b, "feat", axis=0, tiled=True)
    grad_dec = contract_rows(active_b, whole_errors)
    act_terms = dec_scale * lax.dot_general(
        whole_errors, dec_local, (((1,), (1,)), ((), ())), preferred_element_type=jnp.float32
    )
    grad_act = lax.psum(act_terms, "layer")
    grad_pre = jnp.where(preact > 0.0, grad_act, 0.0).astype(jnp.bfloat16)
    tokens_later = lax.all_gather(tok_local, "feat", axis=0, tiled=True)
    grad_enc = contract_rows(tokens_later, grad_pre)
    enc_step = (-LEARN_RATE * enc_scale * grad_enc).astype(jnp.bfloat16)[None]
    dec_step = (-LEARN_RATE * dec_scale * grad_dec).astype(jnp.bfloat16)[None]
    return (enc_step, dec_step)


def solution(mesh):
    in_specs = (
        P("layer", "feat", None),
        P("layer", None, "feat"),
        P("layer", "feat", None),
        P("feat"),
        P("layer", None),
    )
    out_specs = (P("layer", None, "feat"), P("layer", "feat", None))
    return jax.shard_map(body, mesh=mesh, in_specs=in_specs, out_specs=out_specs, check_vma=False)
```

profile of v0, /device:TPU:0, one launch (start us, length us, event | category | flops | bytes accessed | tf_op | source)
XLA Modules:
  0.0 331.6 jit_solution(2923446506743873002)
XLA Ops:
  7.2 0.0 copy-start
  7.2 0.0 all-reduce.3.cloned.1.call-start
  7.2 33.7 %all-gather = bf16[1,512,576]{2,1,0:T(8,128)(2,1)S(1)} all-gather(bf16[1,64,576]{2,1,0:T(8,128)(2,1)} %param.5), channel_id=2, replica_groups=mesh['layer'=4,'feat'=8] {'feat'}, dimensions={1}, use_global_device_ids=true | all-gather | bytes 663552 | tf_op jit(solution)/shard_map/all_gather | solution.py:41
  40.9 0.0 copy-start.6
  40.9 5.4 %fusion.5 = f32[512,2048]{1,0:T(8,128)} fusion(bf16[1,576,2048]{2,1,0:T(8,128)(2,1)} %param.6, bf16[1,512,576]{2,1,0:T(8,128)(2,1)S(1)} %all-gather), kind=kOutput, calls=%fused_computation.11 | convolution fusion | flops 1207959552 | bytes 7143424 | tf_op jit(solution)/shard_map/dot_general | solution.py:24
  46.4 0.0 all-reduce.3.cloned.1.call-update
  46.4 0.0 copy-start.4
  46.4 0.0 copy-start.3
  46.4 0.0 reduce-scatter.2.cloned.1.call-start
  46.5 86.6 %all-reduce.3.cloned.1.call-done = f32[512,2048]{1,0:T(8,128)} async-done(((f32[512,2048]{1,0:T(8,128)}), f32[512,2048]{1,0:T(8,128)}) %all-reduce.3.cloned.1.call-update) | async-done | bytes 4194320 | tf_op jit(solution)/shard_map/psum | solution.py:25
  133.1 0.0 copy-done
  133.1 0.0 copy-done.6
  133.1 5.1 %fusion.10 = f32[512,576]{1,0:T(8,128)} fusion(bf16[1,2048,576]{1,2,0:T(8,128)(2,1)S(1)} %copy-done, f32[512,2048]{1,0:T(8,128)} %all-reduce.3.cloned.1.call-done, f32[2048]{0:T(1024)S(1)} %copy-done.6), kind=kOutput, calls=%fused_computation.16 | convolution fusion | flops 1212448768 | bytes 7741440 | tf_op jit(solution)/shard_map/dot_general | solution.py:28
  138.2 0.0 reduce-scatter.2.cloned.1.call-update
  138.2 0.0 copy-done.4
  138.3 64.6 %reduce-scatter.2.cloned.1.call-done = f32[64,576]{1,0:T(8,128)} async-done(((f32[512,576]{1,0:T(8,128)}), f32[64,576]{1,0:T(8,128)}) %reduce-scatter.2.cloned.1.call-update) | async-done | bytes 147472 | tf_op jit(solution)/shard_map/reduce_scatter | solution.py:27
  202.9 0.0 copy-done.3
  202.9 0.9 fusion.15
  203.8 31.8 %all_gather.8 = bf16[512,576]{1,0:T(8,128)(2,1)S(1)} all-gather(bf16[64,576]{1,0:T(8,128)(2,1)S(1)} %fusion.15), channel_id=1, replica_groups=mesh['layer'=4,'feat'=8] {'feat'}, dimensions={0}, use_global_device_ids=true | all-gather | bytes 663552 | tf_op jit(solution)/shard_map/all_gather | solution.py:34
  235.7 0.0 copy-start.2
  235.7 0.9 copy-done.2
  236.6 3.8 %convolution_multiply_fusion = f32[512,2048]{1,0:T(8,128)} fusion(bf16[512,576]{1,0:T(8,128)(2,1)S(1)} %all_gather.8, bf16[1,2048,576]{1,2,0:T(8,128)(2,1)S(1)} %copy-done), kind=kOutput, calls=%fused_computation.5 | convolution fusion | flops 1209008128 | bytes 7143424 | tf_op jit(solution)/shard_map/dot_general | solution.py:36
  240.3 76.1 %all-reduce.4 = bf16[512,2048]{1,0:T(8,128)(2,1)} all-reduce(f32[512,2048]{1,0:T(8,128)} %convolution_multiply_fusion), channel_id=1, replica_groups=mesh['layer'=4,'feat'=8] {'layer'}, use_global_device_ids=true, to_apply=%region_2.0 | all-reduce | flops 1048576 | bytes 6291456 | tf_op jit(solution)/shard_map/psum | solution.py:39
  316.4 0.0 copy-start.1
  316.4 0.0 copy-start.5
  316.4 5.4 %fusion.1 = bf16[1,2048,576]{1,2,0:T(8,128)(2,1)} fusion(bf16[512,576]{1,0:T(8,128)(2,1)} %copy-done.2, f32[512,2048]{1,0:T(8,128)} %all-reduce.3.cloned.1.call-done, f32[2048]{0:T(1024)S(1)} %copy-done.6), kind=kOutput, calls=%fused_computation.7 | convolution fusion | flops 1214513152 | bytes 7151616 | tf_op jit(solution)/shard_map/dot_general | solution.py:10
  321.8 0.0 copy-done.1
  321.8 0.0 copy-done.5
  321.8 3.0 fusion
  (1 shorter events, 0.0 us)
Async XLA Ops:
  7.2 125.9 %copy-start = (bf16[1,2048,576]{1,2,0:T(8,128)(2,1)S(1)}, bf16[1,2048,576]{1,2,0:T(8,128)(2,1)}, u32[]{:S(2)}) copy-start(bf16[1,2048,576]{1,2,0:T(8,128)(2,1)} %param.7) | copy-start | bytes 7077892
  7.2 125.9 %all-reduce.3.cloned.1.call-start = ((), (), s32[]{:S(2)}) async-start(), calls=%async_computation.1 | async-start | bytes 8388608 | tf_op jit(solution)/shard_map/psum | solution.py:25
  40.9 92.2 %copy-start.6 = (f32[2048]{0:T(1024)S(1)}, f32[2048]{0:T(1024)}, u32[]{:S(2)}) copy-start(f32[2048]{0:T(1024)} %param.8) | copy-start | bytes 24580
  46.4 91.8 %copy-start.4 = (f32[1,576]{1,0:T(1,128)S(1)}, f32[1,576]{1,0:T(1,128)}, u32[]{:S(2)}) copy-start(f32[1,576]{1,0:T(1,128)} %param.9) | copy-start | bytes 6916
  46.4 156.4 %copy-start.3 = (bf16[1,64,576]{2,1,0:T(8,128)(2,1)S(1)}, bf16[1,64,576]{2,1,0:T(8,128)(2,1)}, u32[]{:S(2)}) copy-start(bf16[1,64,576]{2,1,0:T(8,128)(2,1)} %param.5) | copy-start | bytes 221188
  46.4 156.4 %reduce-scatter.2.cloned.1.call-start = ((), (), s32[]{:S(2)}) async-start(), calls=%async_computation.2 | async-start | bytes 1474560 | tf_op jit(solution)/shard_map/reduce_scatter | solution.py:27
  235.7 0.9 copy-start.2
  316.4 5.4 %copy-start.1 = (bf16[512,2048]{1,0:T(8,128)(2,1)S(1)}, bf16[512,2048]{1,0:T(8,128)(2,1)}, u32[]{:S(2)}) copy-start(bf16[512,2048]{1,0:T(8,128)(2,1)} %all-reduce.4) | copy-start | bytes 6291460
  316.4 5.4 %copy-start.5 = (f32[512,2048]{1,0:T(8,128)S(1)}, f32[512,2048]{1,0:T(8,128)}, u32[]{:S(2)}) copy-start(f32[512,2048]{1,0:T(8,128)} %all-reduce.3.cloned.1.call-done) | copy-start | bytes 12582916
Sparse Core Ops, SparseCore 0:
  46.5 86.5 all-reduce.2
  138.3 64.4 reduce-scatter.1
where the time goes:
time: 332 us
  waiting for transfers between devices  151 us (45%)
  blocking collectives  142 us (43%)
  matrix products  22.6 us (7%)
  between operations  14.1 us (4%)
    psum x1, waiting for transfers between devices, body(): preact = enc_scale * lax.psum(partial_value, 'layer') + enc_bias  86.6 us
    psum x1, blocking collectives, body(): grad_act = lax.psum(act_terms, 'layer')  76.1 us
    reduce_scatter x1, waiting for transfers between devices, body(): lax.psum_scatter(dec_scale * jnp.dot(active_b, dec_local, preferred_eleme...  64.6 us
    all_gather x1, blocking collectives, body(): tokens_later = lax.all_gather(tok_local, 'feat', axis=0, tiled=True)  33.7 us
    all_gather x1, blocking collectives, body(): whole_errors = lax.all_gather(error_b, 'feat', axis=0, tiled=True)  31.8 us
    dot_general x2, matrix products, contract_rows(): lax.dot_general(left, right, (((0,), (0,)), ((), ())), preferred_element_...  8.34 us
  transfers between devices with their start and end apart: 2, of which 2 were waited for; matrix products, arithmetic and copies ran while one was open for 0% of the time, Pallas kernels for 0%

commit v1 on v0

--- a/solution.py
+++ b/solution.py
@@ -1,15 +1,263 @@
+import functools
+
 import jax
 import jax.numpy as jnp
 from jax import lax
+from jax.experimental import pallas as pl
+from jax.experimental.pallas import tpu as pltpu
 from jax.sharding import PartitionSpec as P
 
 LEARN_RATE = 4.0
+MESH = pl.DeviceIdType.MESH
+F32 = jnp.float32
+BF16 = jnp.bfloat16
+
+STAGES = (
+    ("partial", -6.0),
+    ("pair_sum", 1.0),
+    ("activate", 11.0),
+    ("pass_active", 18.0),
+    ("decode", 19.5),
+    ("fold_y", 22.0),
+    ("fold_z", 24.5),
+    ("pass_error", 26.5),
+    ("grad", 29.0),
+    ("grad_pair", 31.0),
+    ("mask", 40.0),
+)
+PERIOD = 8.0
 
 
 def contract_rows(left, right):
-    return lax.dot_general(
-        left, right, (((0,), (0,)), ((), ())), preferred_element_type=jnp.float32
-    )
+    return lax.dot_general(left, right, (((0,), (0,)), ((), ())), preferred_element_type=F32)
+
+
+def contract_columns(left, right):
+    return lax.dot_general(left, right, (((1,), (1,)), ((), ())), preferred_element_type=F32)
+
+
+def kernel(chunks, rows, quarter, enc_scale, dec_scale, tok_ref, enc_ref, dec_ref, bias_ref, dbias_ref,
+           enc_out, dec_out, tok, psend, prec, pown, xsend, xrec, act, rpart, yrec, zsend, zrec, err,
+           gsend, grec, gown, xgsend, xgrec, gp, sends, recvs):
+    layer, feat = lax.axis_index("layer"), lax.axis_index("feat")
+    xi, core = layer // 2, layer % 2
+    zi, yi = feat // 2, feat % 2
+    pair_dev = (xi * 2 + (1 - core), feat)
+    x_dev = ((1 - xi) * 2 + core, feat)
+    y_dev = (layer, zi * 2 + (1 - yi))
+
+    def z_at(step):
+        return lax.rem(zi + step + 4, 4)
+
+    def z_dev(step):
+        return (layer, z_at(step) * 2 + yi)
+
+    barrier = pltpu.get_barrier_semaphore()
+    peers = [pair_dev, x_dev, y_dev, z_dev(1), z_dev(2), z_dev(3)]
+    for peer in peers:
+        pl.semaphore_signal(barrier, inc=1, device_id=peer, device_id_type=MESH)
+    pl.semaphore_wait(barrier, len(peers))
+
+    started = []
+
+    def copy(c, kind, src, dst, dev):
+        return pltpu.make_async_remote_copy(
+            src_ref=src, dst_ref=dst, send_sem=sends.at[c, kind], recv_sem=recvs.at[c, kind],
+            device_id=dev, device_id_type=MESH)
+
+    def send(c, kind, src, dst, dev):
+        moving = copy(c, kind, src, dst, dev)
+        moving.start()
+        started.append(moving)
+
+    def arrive(c, kind, dst, dev):
+        copy(c, kind, dst, dst, dev).wait_recv()
+
+    def gather_begin(c, base, buf):
+        own = buf.at[c, feat]
+        send(c, base, own, own, y_dev)
+        for step in (1, 2, 3):
+            send(c, base + step, own, own, z_dev(step))
+
+    def gather_pass(c, base, buf):
+        for step in (1, 3, 2):
+            slot = buf.at[c, z_at(-step) * 2 + yi]
+            arrive(c, base + step, slot, z_dev(-step))
+            send(c, base + 3 + step, slot, slot, y_dev)
+
+    def gather_end(c, base, buf):
+        arrive(c, base, buf.at[c, zi * 2 + (1 - yi)], y_dev)
+        for step in (1, 2, 3):
+            arrive(c, base + 3 + step, buf.at[c, z_at(-step) * 2 + (1 - yi)], y_dev)
+
+    TOK, ERR, PAIR, XP, XA, CA, CB, YR, ZR, GP, GX, GM = 0, 7, 14, 15, 16, 17, 18, 19, 20, 23, 24, 25
+
+    def columns(q):
+        return pl.ds(pl.multiple_of(q * quarter, quarter), quarter)
+
+    def partial(c):
+        if c == 0:
+            gather_pass(0, TOK, tok)
+        gather_end(c, TOK, tok)
+        if c + 1 < chunks:
+            gather_pass(c + 1, TOK, tok)
+
+        @pl.loop(0, 2)
+        def _(j):
+            x = tok[c].reshape(8 * rows, -1)
+            psend[c, j] = jnp.dot(x, enc_ref[:, columns((1 - core) * 2 + j)], preferred_element_type=F32)
+
+        send(c, PAIR, psend.at[c], prec.at[c], pair_dev)
+
+        @pl.loop(0, 2)
+        def _(j):
+            x = tok[c].reshape(8 * rows, -1)
+            pown[c, j] = jnp.dot(x, enc_ref[:, columns(core * 2 + j)], preferred_element_type=F32)
+
+    def pair_sum(c):
+        arrive(c, PAIR, prec.at[c], pair_dev)
+        xsend[c] = pown[c, 1 - xi] + prec[c, 1 - xi]
+        send(c, XP, xsend.at[c], xrec.at[c], x_dev)
+
+    def activate(c):
+        arrive(c, XP, xrec.at[c], x_dev)
+        total = pown[c, xi] + prec[c, xi] + xrec[c]
+        mine = core * 2 + xi
+        preact = enc_scale * total + bias_ref[mine]
+        act[c, mine] = jnp.maximum(preact, 0.0).astype(BF16)
+        send(c, XA, act.at[c, mine], act.at[c, mine], x_dev)
+        send(c, CA, act.at[c, mine], act.at[c, mine], pair_dev)
+
+    def pass_active(c):
+        other = act.at[c, core * 2 + (1 - xi)]
+        arrive(c, XA, other, x_dev)
+        send(c, CB, other, other, pair_dev)
+
+    def decode(c):
+        arrive(c, CA, act.at[c, (1 - core) * 2 + xi], pair_dev)
+        arrive(c, CB, act.at[c, (1 - core) * 2 + (1 - xi)], pair_dev)
+        part = contract_columns(act[c, 0], dec_ref[:, 0:quarter])
+        for q in range(1, 4):
+            part = part + contract_columns(act[c, q], dec_ref[:, q * quarter:(q + 1) * quarter])
+        part = (dec_scale * part).astype(BF16).reshape(8, rows, -1)
+        for f in range(8):
+            rpart[c, f % 2, f // 2] = part[f]
+        send(c, YR, rpart.at[c, 1 - yi], yrec.at[c], y_dev)
+
+    def fold_y(c):
+        arrive(c, YR, yrec.at[c], y_dev)
+        zsend[c] = (rpart[c, yi].astype(F32) + yrec[c].astype(F32)).astype(BF16)
+        for step in (1, 2, 3):
+            send(c, ZR + step - 1, zsend.at[c, z_at(step)], zrec.at[c, step - 1], z_dev(step))
+
+    def fold_z(c):
+        recon = rpart[c, yi, zi].astype(F32) + yrec[c, zi].astype(F32)
+        for step in (1, 2, 3):
+            arrive(c, ZR + step - 1, zrec.at[c, step - 1], z_dev(-step))
+            recon = recon + zrec[c, step - 1].astype(F32)
+        own = tok_ref[c * rows:(c + 1) * rows, :].astype(F32)
+        err[c, feat] = (recon + dbias_ref[...] - own).astype(BF16)
+        gather_begin(c, ERR, err)
+
+    def pass_error(c):
+        gather_pass(c, ERR, err)
+
+    def grad(c):
+        gather_end(c, ERR, err)
+
+        @pl.loop(0, 2)
+        def _(j):
+            e = err[c].reshape(8 * rows, -1)
+            g = jnp.dot(e, dec_ref[:, columns((1 - core) * 2 + j)], preferred_element_type=F32)
+            gsend[c, j] = (dec_scale * g).astype(BF16)
+
+        send(c, GP, gsend.at[c], grec.at[c], pair_dev)
+
+        @pl.loop(0, 2)
+        def _(j):
+            e = err[c].reshape(8 * rows, -1)
+            g = jnp.dot(e, dec_ref[:, columns(core * 2 + j)], preferred_element_type=F32)
+            gown[c, j] = dec_scale * g
+
+    def grad_pair(c):
+        arrive(c, GP, grec.at[c], pair_dev)
+        for j in range(2):
+            both = gown[c, j] + grec[c, j].astype(F32)
+            gown[c, j] = both
+            xgsend[c, j] = both.astype(BF16)
+        send(c, GX, xgsend.at[c], xgrec.at[c], x_dev)
+
+    def mask(c):
+        arrive(c, GX, xgrec.at[c], x_dev)
+        for j in range(2):
+            whole = gown[c, j] + xgrec[c, j].astype(F32)
+            lit = act[c, core * 2 + j].astype(F32) > 0.0
+            gp[c, core * 2 + j] = jnp.where(lit, whole, 0.0).astype(BF16)
+        own = gp.at[c, pl.ds(core * 2, 2)]
+        send(c, GM, own, own, pair_dev)
+
+    for c in range(chunks):
+        tok[c, feat] = tok_ref[c * rows:(c + 1) * rows, :]
+        gather_begin(c, TOK, tok)
+    stages = dict(partial=partial, pair_sum=pair_sum, activate=activate, pass_active=pass_active, decode=decode,
+                  fold_y=fold_y, fold_z=fold_z, pass_error=pass_error, grad=grad, grad_pair=grad_pair, mask=mask)
+    order = sorted((due + c * PERIOD, i, c, name) for i, (name, due) in enumerate(STAGES) for c in range(chunks))
+    last_grad = max(i for i, item in enumerate(order) if item[3] == "grad_pair")
+    for i, (_, _, c, name) in enumerate(order):
+        stages[name](c)
+        if i == last_grad:
+            @pl.loop(0, 4)
+            def _(q):
+                left = err[...].reshape(chunks * 8 * rows, -1)
+                right = jnp.concatenate([act[c, q] for c in range(chunks)], axis=0)
+                dec_out[:, columns(q)] = (-LEARN_RATE * dec_scale * contract_rows(left, right)).astype(BF16)
+
+    for c in range(chunks):
+        arrive(c, GM, gp.at[c, pl.ds((1 - core) * 2, 2)], pair_dev)
+
+    @pl.loop(0, 4)
+    def _(q):
+        left = tok[...].reshape(chunks * 8 * rows, -1)
+        right = jnp.concatenate([gp[c, q] for c in range(chunks)], axis=0)
+        enc_out[:, columns(q)] = (-LEARN_RATE * enc_scale * contract_rows(left, right)).astype(BF16)
+
+    for moving in started:
+        moving.wait_send()
+
+
+def fused(layer_acts, enc_weight, dec_weight, enc_bias, dec_bias):
+    tokens, width = layer_acts.shape[1:]
+    features = enc_weight.shape[2]
+    chunks, quarter = 4, features // 4
+    rows = tokens // chunks
+    enc_scale = (lax.axis_size("layer") * width) ** (-0.5)
+    dec_scale = (features * lax.axis_size("feat")) ** (-0.5)
+    whole = 8 * rows
+    vmem = pl.BlockSpec(memory_space=pltpu.VMEM)
+    half32 = pltpu.VMEM((chunks, 2, whole, quarter), F32)
+    half16 = pltpu.VMEM((chunks, 2, whole, quarter), BF16)
+    quarter32 = pltpu.VMEM((chunks, whole, quarter), F32)
+    full16 = pltpu.VMEM((chunks, 4, whole, quarter), BF16)
+    blocks = pltpu.VMEM((chunks, 8, rows, width), BF16)
+    enc_step, dec_step = pl.pallas_call(
+        functools.partial(kernel, chunks, rows, quarter, enc_scale, dec_scale),
+        out_shape=[jax.ShapeDtypeStruct((width, features), BF16)] * 2,
+        in_specs=[vmem] * 5,
+        out_specs=[vmem] * 2,
+        scratch_shapes=[
+            blocks, half32, half32, half32, quarter32, quarter32, full16,
+            pltpu.VMEM((chunks, 2, 4, rows, width), BF16),
+            pltpu.VMEM((chunks, 4, rows, width), BF16),
+            pltpu.VMEM((chunks, 4, rows, width), BF16),
+            pltpu.VMEM((chunks, 3, rows, width), BF16),
+            blocks, half16, half16, half32, half16, half16, full16,
+            pltpu.SemaphoreType.DMA((chunks, 26)),
+            pltpu.SemaphoreType.DMA((chunks, 26)),
+        ],
+        compiler_params=pltpu.CompilerParams(
+            collective_id=0, has_side_effects=True, vmem_limit_bytes=58 * 2**20),
+    )(layer_acts[0], enc_weight[0], jnp.swapaxes(dec_weight[0], 0, 1), enc_bias.reshape(4, 1, quarter), dec_bias)
+    return enc_step[None], jnp.swapaxes(dec_step, 0, 1)[None]
 
 
 def body(layer_acts, enc_weight, dec_weight, enc_bias, dec_bias):
@@ -33,13 +281,10 @@
     error_b = (recon + dec_bias[0] - tok_local.astype(jnp.float32)).astype(jnp.bfloat16)
     whole_errors = lax.all_gather(error_b, "feat", axis=0, tiled=True)
     grad_dec = contract_rows(active_b, whole_errors)
-    act_terms = dec_scale * lax.dot_general(
-        whole_errors, dec_local, (((1,), (1,)), ((), ())), preferred_element_type=jnp.float32
-    )
+    act_terms = dec_scale * contract_columns(whole_errors, dec_local)
     grad_act = lax.psum(act_terms, "layer")
     grad_pre = jnp.where(preact > 0.0, grad_act, 0.0).astype(jnp.bfloat16)
-    tokens_later = lax.all_gather(tok_local, "feat", axis=0, tiled=True)
-    grad_enc = contract_rows(tokens_later, grad_pre)
+    grad_enc = contract_rows(whole_tokens, grad_pre)
     enc_step = (-LEARN_RATE * enc_scale * grad_enc).astype(jnp.bfloat16)[None]
     dec_step = (-LEARN_RATE * dec_scale * grad_dec).astype(jnp.bfloat16)[None]
     return (enc_step, dec_step)
@@ -54,4 +299,5 @@
         P("layer", None),
     )
     out_specs = (P("layer", None, "feat"), P("layer", "feat", None))
-    return jax.shard_map(body, mesh=mesh, in_specs=in_specs, out_specs=out_specs, check_vma=False)
+    run = fused if (mesh.shape["layer"], mesh.shape["feat"]) == (4, 8) else body
+    return jax.shard_map(run, mesh=mesh, in_specs=in_specs, out_specs=out_specs, check_vma=False)

time: 332 us -> 110 us (0.33)
  waiting for transfers between devices: 151 us -> 0 us
  blocking collectives: 142 us -> 0 us
  Pallas kernels: 0 us -> 104 us
  matrix products: 22.6 us -> 0 us
  between operations: 14.1 us -> 0.65 us
  local copies, waits for them, and re-layouts: 0.94 us -> 4.92 us
    pallas_call x0 -> x1, Pallas kernels: none -> 104 us  [fused(): pl.pallas_call(functools.partial(kernel, chunks, rows, quarter, enc_scale...]
    psum x1 -> x0, waiting for transfers between devices: 86.6 us -> none  [body(): preact = enc_scale * lax.psum(partial_value, 'layer') + enc_bias]
    psum x1 -> x0, blocking collectives: 76.1 us -> none  [body(): grad_act = lax.psum(act_terms, 'layer')]
    all_gather x2 -> x0, blocking collectives: 65.6 us -> none  [the longest x1 33.7 us: body(): tokens_later = lax.all_gather(tok_local, 'feat', axis=0, tiled=True)]
    reduce_scatter x1 -> x0, waiting for transfers between devices: 64.6 us -> none  [body(): lax.psum_scatter(dec_scale * jnp.dot(active_b, dec_local, preferred_eleme...]
    dot_general x5 -> x0, matrix products: 22.6 us -> none  [the longest x2 8.34 us: contract_rows(): lax.dot_general(left, right, (((0,), (0,)), ((), ())), preferred_element_...]
    unnamed x14 -> x4, local copies, waits for them, and re-layouts: 0.94 us -> 4.92 us
  transfers between devices with their start and end apart: 2 -> 0, of which waited for: 2 -> 0; matrix products, arithmetic and copies ran while one was open for 0% -> 0% of each run, Pallas kernels for 0% -> 0%
where the time goes in v1:
time: 110 us
  Pallas kernels  104 us (95%)
  local copies, waits for them, and re-layouts  4.92 us (4%)
    pallas_call x1, Pallas kernels, fused(): pl.pallas_call(functools.partial(kernel, chunks, rows, quarter, enc_scale...  104 us
    unnamed x4, local copies, waits for them, and re-layouts  4.92 us

profile of v1, /device:TPU:0, one launch (start us, length us, event | category | flops | bytes accessed | tf_op | source)
XLA Modules:
  0.0 110.0 jit_solution(17529732755657858641)
XLA Ops:
  0.6 104.4 %shard_map.68 = (bf16[576,2048]{1,0:T(8,128)(2,1)}, bf16[576,2048]{1,0:T(8,128)(2,1)}) custom-call(bf16[64,576]{1,0:T(8,128)(2,1)} %bitcast.14, bf16[576,2048]{1,0:T(8,128)(2,1)} %bitcast.10, bf16[576,2048]{1,0:T(8,128)(2,1)} %bitcast.11, f32[4,1,512]{2,1,0:T(1,128)} %bitcast.15, f32[1,576]{1,0:T(1,128)} %dbias_ref.1), custom_call_target="tpu_custom_call" | custom-call | tf_op jit(solution)/shard_map/pallas_call | solution.py:242
  105.1 0.0 copy-start
  105.1 3.5 %copy.9 = bf16[1,576,2048]{2,1,0:T(8,128)(2,1)} copy(bf16[1,576,2048]{2,1,0:T(8,128)(2,1)} %bitcast.13) | data formatting | bytes 4718592
  108.6 0.0 copy-done
  108.6 1.4 %copy.10 = bf16[1,2048,576]{1,2,0:T(8,128)(2,1)} copy(bf16[1,2048,576]{1,2,0:T(8,128)(2,1)S(1)} %bitcast.12) | data formatting | bytes 4718592
Async XLA Ops:
  105.1 3.5 %copy-start = (bf16[576,2048]{1,0:T(8,128)(2,1)S(1)}, bf16[576,2048]{1,0:T(8,128)(2,1)}, u32[]{:S(2)}) copy-start(bf16[576,2048]{1,0:T(8,128)(2,1)} %get-tuple-element.5) | copy-start | bytes 7077892

commit v2 on v1

v2 whole, which is shorter than its diff:
```python
import functools

import jax
import jax.numpy as jnp
from jax import lax
from jax.experimental import pallas as pl
from jax.experimental.pallas import tpu as pltpu
from jax.sharding import PartitionSpec as P

LEARN_RATE = 4.0
MESH = pl.DeviceIdType.MESH
F32 = jnp.float32
BF16 = jnp.bfloat16

ORDER = (
    ("partial", 0), ("pair_sum", 0), ("partial", 1), ("pair_sum", 1),
    ("partial", 2), ("activate", 0), ("pair_sum", 2), ("activate", 1),
    ("pass_active", 0), ("partial", 3), ("decode", 0), ("activate", 2),
    ("pass_active", 1), ("pair_sum", 3), ("fold", 0), ("pass_active", 2),
    ("decode", 1), ("decode", 2), ("activate", 3), ("fold", 1),
    ("grad", 0), ("fold", 2), ("grad_pair", 0), ("pass_active", 3),
    ("grad", 1), ("decode", 3), ("grad_pair", 1), ("grad", 2),
    ("mask", 0), ("fold", 3), ("grad_pair", 2), ("grad", 3),
    ("grad_pair", 3), ("mask", 2), ("mask", 1), ("dec_all", 2),
    ("mask", 3),
)


def contract_rows(left, right):
    return lax.dot_general(left, right, (((0,), (0,)), ((), ())), preferred_element_type=F32)


def contract_columns(left, right):
    return lax.dot_general(left, right, (((1,), (1,)), ((), ())), preferred_element_type=F32)


def kernel(chunks, rows, quarter, enc_scale, dec_scale, tok_ref, enc_hbm, dec_hbm, bias_ref, dbias_ref,
           tok, gp, dec_out, enc_ref, dec_ref, dec_acc, psend, prec, pown, xsend, xrec, act, rpart, rrec, err,
           gsend, grec, gown, xgsend, xgrec, loads, sends, recvs):
    layer, feat = lax.axis_index("layer"), lax.axis_index("feat")
    xi, core = layer // 2, layer % 2
    pair_dev = (xi * 2 + (1 - core), feat)
    x_dev = ((1 - xi) * 2 + core, feat)
    steps = range(1, 8)

    load_enc = pltpu.make_async_copy(enc_hbm, enc_ref, loads.at[0])
    load_dec = pltpu.make_async_copy(dec_hbm, dec_ref, loads.at[1])
    load_enc.start()
    load_dec.start()

    def feat_at(step):
        return lax.rem(feat + step + 8, 8)

    def feat_dev(step):
        return (layer, feat_at(step))

    barrier = pltpu.get_barrier_semaphore()
    peers = [pair_dev, x_dev] + [feat_dev(step) for step in steps]
    for peer in peers:
        pl.semaphore_signal(barrier, inc=1, device_id=peer, device_id_type=MESH)
    for c in range(chunks):
        tok[c, feat] = tok_ref[c * rows:(c + 1) * rows, :]
    pl.semaphore_wait(barrier, len(peers))

    started = []

    def copy(c, kind, src, dst, dev):
        return pltpu.make_async_remote_copy(
            src_ref=src, dst_ref=dst, send_sem=sends.at[c, kind], recv_sem=recvs.at[c, kind],
            device_id=dev, device_id_type=MESH)

    def send(c, kind, src, dst, dev):
        moving = copy(c, kind, src, dst, dev)
        moving.start()
        started.append(moving)

    def arrive(c, kind, dst, dev):
        copy(c, kind, dst, dst, dev).wait_recv()

    def gather_begin(c, base, buf):
        own = buf.at[c, feat]
        for step in (4, 3, 5, 2, 6, 1, 7):
            send(c, base + step - 1, own, own, feat_dev(step))

    def gather_end(c, base, buf):
        for step in steps:
            arrive(c, base + step - 1, buf.at[c, feat_at(-step)], feat_dev(-step))

    TOK, ERR, RS, PAIR, XP, XA, CA, CB, GP, GX, GM = 0, 7, 14, 21, 23, 24, 25, 26, 27, 29, 31

    def columns(q):
        return pl.ds(pl.multiple_of(q * quarter, quarter), quarter)

    halves = ((0, 1 - xi), (1, xi))

    def partial(c):
        gather_end(c, TOK, tok)
        if c == 0:
            load_enc.wait()
        x = tok[c].reshape(8 * rows, -1)
        for i, j in halves:
            psend[c, i] = jnp.dot(x, enc_ref[:, columns((1 - core) * 2 + j)], preferred_element_type=F32)
            send(c, PAIR + i, psend.at[c, i], prec.at[c, i], pair_dev)
        for i, j in halves:
            pown[c, i] = jnp.dot(x, enc_ref[:, columns(core * 2 + j)], preferred_element_type=F32)

    def pair_sum(c):
        arrive(c, PAIR, prec.at[c, 0], pair_dev)
        xsend[c] = pown[c, 0] + prec[c, 0]
        send(c, XP, xsend.at[c], xrec.at[c], x_dev)

    def activate(c):
        arrive(c, PAIR + 1, prec.at[c, 1], pair_dev)
        arrive(c, XP, xrec.at[c], x_dev)
        total = pown[c, 1] + prec[c, 1] + xrec[c]
        mine = core * 2 + xi
        preact = enc_scale * total + bias_ref[mine]
        act[c, mine] = jnp.maximum(preact, 0.0).astype(BF16)
        send(c, XA, act.at[c, mine], act.at[c, mine], x_dev)
        send(c, CA, act.at[c, mine], act.at[c, mine], pair_dev)

    def pass_active(c):
        other = act.at[c, core * 2 + (1 - xi)]
        arrive(c, XA, other, x_dev)
        send(c, CB, other, other, pair_dev)

    def decode(c):
        if c == 0:
            load_dec.wait()
        arrive(c, CA, act.at[c, (1 - core) * 2 + xi], pair_dev)
        arrive(c, CB, act.at[c, (1 - core) * 2 + (1 - xi)], pair_dev)
        part = contract_columns(act[c, 0], dec_ref[:, 0:quarter])
        for q in range(1, 4):
            part = part + contract_columns(act[c, q], dec_ref[:, q * quarter:(q + 1) * quarter])
        rpart[c] = (dec_scale * part).astype(BF16).reshape(8, rows, -1)
        for step in (4, 3, 5, 2, 6, 1, 7):
            send(c, RS + step - 1, rpart.at[c, feat_at(step)], rrec.at[c, step - 1], feat_dev(step))

    def fold(c):
        recon = rpart[c, feat].astype(F32)
        for step in steps:
            arrive(c, RS + step - 1, rrec.at[c, step - 1], feat_dev(-step))
            recon = recon + rrec[c, step - 1].astype(F32)
        own = tok_ref[c * rows:(c + 1) * rows, :].astype(F32)
        err[c, feat] = (recon + dbias_ref[...] - own).astype(BF16)
        gather_begin(c, ERR, err)

    def grad(c):
        gather_end(c, ERR, err)
        e = err[c].reshape(8 * rows, -1)
        for j in range(2):
            g = jnp.dot(e, dec_ref[:, columns((1 - core) * 2 + j)], preferred_element_type=F32)
            gsend[c, j] = (dec_scale * g).astype(BF16)
            send(c, GP + j, gsend.at[c, j], grec.at[c, j], pair_dev)
        for j in range(2):
            g = jnp.dot(e, dec_ref[:, columns(core * 2 + j)], preferred_element_type=F32)
            gown[c, j] = dec_scale * g

    def grad_pair(c):
        for j in range(2):
            arrive(c, GP + j, grec.at[c, j], pair_dev)
            both = gown[c, j] + grec[c, j].astype(F32)
            gown[c, j] = both
            xgsend[c, j] = both.astype(BF16)
            send(c, GX + j, xgsend.at[c, j], xgrec.at[c, j], x_dev)

    def mask(c):
        for j in range(2):
            arrive(c, GX + j, xgrec.at[c, j], x_dev)
            whole = gown[c, j] + xgrec[c, j].astype(F32)
            q = core * 2 + j
            lit = act[c, q].astype(F32) > 0.0
            gp[c, q] = jnp.where(lit, whole, 0.0).astype(BF16)
            send(c, GM + j, gp.at[c, q], gp.at[c, q], pair_dev)

    store_dec = pltpu.make_async_copy(dec_acc, dec_out, loads.at[2])

    def dec_all(_):
        @pl.loop(0, 4)
        def _(q):
            left = err[...].reshape(chunks * 8 * rows, -1)
            right = jnp.concatenate([act[c, q] for c in range(chunks)], axis=0)
            dec_acc[:, columns(q)] = (-LEARN_RATE * dec_scale * contract_rows(left, right)).astype(BF16)

        store_dec.start()

    for c in range(chunks):
        gather_begin(c, TOK, tok)
    stages = dict(partial=partial, pair_sum=pair_sum, activate=activate, pass_active=pass_active, decode=decode,
                  fold=fold, grad=grad, grad_pair=grad_pair, mask=mask, dec_all=dec_all)
    for name, c in ORDER:
        stages[name](c)
    for c in range(chunks):
        for j in range(2):
            arrive(c, GM + j, gp.at[c, (1 - core) * 2 + j], pair_dev)
    store_dec.wait()
    for moving in started:
        moving.wait_send()


def finish(scale, tok_ref, gp_ref, dec_ref, enc_out, dec_out):
    chunks = tok_ref.shape[0]
    left = tok_ref[...].reshape(-1, tok_ref.shape[3])
    right = jnp.concatenate([gp_ref[c, 0] for c in range(chunks)], axis=0)
    enc_out[...] = (scale * contract_rows(left, right)).astype(BF16)
    dec_out[...] = dec_ref[...]


def fused(layer_acts, enc_weight, dec_weight, enc_bias, dec_bias):
    tokens, width = layer_acts.shape[1:]
    features = enc_weight.shape[2]
    chunks, quarter = 4, features // 4
    rows = tokens // chunks
    enc_scale = (lax.axis_size("layer") * width) ** (-0.5)
    dec_scale = (features * lax.axis_size("feat")) ** (-0.5)
    whole = 8 * rows
    vmem = pl.BlockSpec(memory_space=pltpu.VMEM)
    anywhere = pl.BlockSpec(memory_space=pl.ANY)
    half32 = pltpu.VMEM((chunks, 2, whole, quarter), F32)
    half16 = pltpu.VMEM((chunks, 2, whole, quarter), BF16)
    quarter32 = pltpu.VMEM((chunks, whole, quarter), F32)
    full16 = pltpu.VMEM((chunks, 4, whole, quarter), BF16)
    blocks = pltpu.VMEM((chunks, 8, rows, width), BF16)
    weights = pltpu.VMEM((width, features), BF16)
    step_shape = jax.ShapeDtypeStruct((width, features), BF16)
    tok, gp, dec_step = pl.pallas_call(
        functools.partial(kernel, chunks, rows, quarter, enc_scale, dec_scale),
        out_shape=[
            jax.ShapeDtypeStruct((chunks, 8, rows, width), BF16),
            jax.ShapeDtypeStruct((chunks, 4, whole, quarter), BF16),
            step_shape,
        ],
        in_specs=[vmem, anywhere, anywhere, vmem, vmem],
        out_specs=[vmem, vmem, anywhere],
        scratch_shapes=[
            weights, weights, weights, half32, half32, half32, quarter32, quarter32, full16, blocks,
            pltpu.VMEM((chunks, 7, rows, width), BF16),
            blocks, half16, half16, half32, half16, half16,
            pltpu.SemaphoreType.DMA((3,)),
            pltpu.SemaphoreType.DMA((chunks, 33)),
            pltpu.SemaphoreType.DMA((chunks, 33)),
        ],
        compiler_params=pltpu.CompilerParams(
            collective_id=0, has_side_effects=True, vmem_limit_bytes=56 * 2**20),
    )(layer_acts[0], enc_weight[0], jnp.swapaxes(dec_weight[0], 0, 1), enc_bias.reshape(4, 1, quarter), dec_bias)
    slab = pl.BlockSpec((width, quarter), lambda q: (0, q))
    enc_step, dec_step = pl.pallas_call(
        functools.partial(finish, -LEARN_RATE * enc_scale),
        out_shape=[step_shape, step_shape],
        grid=(4,),
        in_specs=[
            pl.BlockSpec((chunks, 8, rows, width), lambda q: (0, 0, 0, 0)),
            pl.BlockSpec((chunks, 1, whole, quarter), lambda q: (0, q, 0, 0)),
            slab,
        ],
        out_specs=[slab, slab],
        compiler_params=pltpu.CompilerParams(vmem_limit_bytes=60 * 2**20),
    )(tok, gp, dec_step)
    return enc_step[None], jnp.swapaxes(dec_step, 0, 1)[None]


def body(layer_acts, enc_weight, dec_weight, enc_bias, dec_bias):
    tok_local = layer_acts[0]
    enc_local = enc_weight[0]
    dec_local = dec_weight[0]
    model_width = enc_local.shape[0]
    slab_width = enc_local.shape[1]
    enc_scale = (layer_acts.shape[0] * lax.axis_size("layer") * model_width) ** (-0.5)
    dec_scale = (slab_width * lax.axis_size("feat")) ** (-0.5)
    whole_tokens = lax.all_gather(tok_local, "feat", axis=0, tiled=True)
    partial_value = jnp.dot(whole_tokens, enc_local, preferred_element_type=jnp.float32)
    preact = enc_scale * lax.psum(partial_value, "layer") + enc_bias
    active_b = jnp.maximum(preact, 0.0).astype(jnp.bfloat16)
    recon = lax.psum_scatter(
        dec_scale * jnp.dot(active_b, dec_local, preferred_element_type=jnp.float32),
        "feat",
        scatter_dimension=0,
        tiled=True,
    )
    error_b = (recon + dec_bias[0] - tok_local.astype(jnp.float32)).astype(jnp.bfloat16)
    whole_errors = lax.all_gather(error_b, "feat", axis=0, tiled=True)
    grad_dec = contract_rows(active_b, whole_errors)
    act_terms = dec_scale * contract_columns(whole_errors, dec_local)
    grad_act = lax.psum(act_terms, "layer")
    grad_pre = jnp.where(preact > 0.0, grad_act, 0.0).astype(jnp.bfloat16)
    grad_enc = contract_rows(whole_tokens, grad_pre)
    enc_step = (-LEARN_RATE * enc_scale * grad_enc).astype(jnp.bfloat16)[None]
    dec_step = (-LEARN_RATE * dec_scale * grad_dec).astype(jnp.bfloat16)[None]
    return (enc_step, dec_step)


def solution(mesh):
    in_specs = (
        P("layer", "feat", None),
        P("layer", None, "feat"),
        P("layer", "feat", None),
        P("feat"),
        P("layer", None),
    )
    out_specs = (P("layer", None, "feat"), P("layer", "feat", None))
    run = fused if (mesh.shape["layer"], mesh.shape["feat"]) == (4, 8) else body
    return jax.shard_map(run, mesh=mesh, in_specs=in_specs, out_specs=out_specs, check_vma=False)
```

time: 110 us -> 91.9 us (0.84)
  Pallas kernels: 104 us -> 91.1 us
  local copies, waits for them, and re-layouts: 4.92 us -> 0 us
    pallas_call x1, Pallas kernels: 104 us -> 85 us  [fused(): pl.pallas_call(functools.partial(kernel, chunks, rows, quarter, enc_scale...]
    pallas_call x0 -> x1, Pallas kernels: none -> 6.04 us  [fused(): pl.pallas_call(functools.partial(finish, -LEARN_RATE * enc_scale), out_sh...]
    unnamed x4 -> x0, local copies, waits for them, and re-layouts: 4.92 us -> none
where the time goes in v2:
time: 91.9 us; the launch traced here: 91.7 us
  Pallas kernels  91.1 us (99%)
    pallas_call x1, Pallas kernels, fused(): pl.pallas_call(functools.partial(kernel, chunks, rows, quarter, enc_scale...  85 us
    pallas_call x1, Pallas kernels, fused(): pl.pallas_call(functools.partial(finish, -LEARN_RATE * enc_scale), out_sh...  6.04 us

profile of v2, /device:TPU:0, one launch (start us, length us, event | category | flops | bytes accessed | tf_op | source)
XLA Modules:
  0.0 91.7 jit_solution(14833378889353304764)
XLA Ops:
  0.6 85.0 %shard_map.68 = (bf16[4,8,16,576]{3,2,1,0:T(8,128)(2,1)}, bf16[4,4,128,512]{3,2,1,0:T(8,128)(2,1)}, bf16[576,2048]{1,0:T(8,128)(2,1)}) custom-call(bf16[64,576]{1,0:T(8,128)(2,1)} %bitcast.12, bf16[576,2048]{1,0:T(8,128)(2,1)} %bitcast.10, bf16[576,2048]{1,0:T(8,128)(2,1)} %bitcast.11, f32[4,1,512]{2,1,0:T(1,128)} %bitcast.13, f32[1,576]{1,0:T(1,128)} %dbias_ref.1), custom_call_target="tpu_custom_call" | custom-call | tf_op jit(solution)/shard_map/pallas_call | solution.py:226
  85.7 6.0 %shard_map.69 = (bf16[576,2048]{1,0:T(8,128)(2,1)}, bf16[576,2048]{1,0:T(8,128)(2,1)}) custom-call(bf16[4,8,16,576]{3,2,1,0:T(8,128)(2,1)} %get-tuple-element.7.tok_ref, bf16[4,4,128,512]{3,2,1,0:T(8,128)(2,1)} %get-tuple-element.8.gp_ref, bf16[576,2048]{1,0:T(8,128)(2,1)} %get-tuple-element.9.dec_ref), custom_call_target="tpu_custom_call" | custom-call | tf_op jit(solution)/shard_map/pallas_call | solution.py:247

commit v3 on v2

--- a/solution.py
+++ b/solution.py
@@ -13,16 +13,17 @@
 BF16 = jnp.bfloat16
 
 ORDER = (
-    ("partial", 0), ("pair_sum", 0), ("partial", 1), ("pair_sum", 1),
-    ("partial", 2), ("activate", 0), ("pair_sum", 2), ("activate", 1),
-    ("pass_active", 0), ("partial", 3), ("decode", 0), ("activate", 2),
-    ("pass_active", 1), ("pair_sum", 3), ("fold", 0), ("pass_active", 2),
-    ("decode", 1), ("decode", 2), ("activate", 3), ("fold", 1),
-    ("grad", 0), ("fold", 2), ("grad_pair", 0), ("pass_active", 3),
-    ("grad", 1), ("decode", 3), ("grad_pair", 1), ("grad", 2),
-    ("mask", 0), ("fold", 3), ("grad_pair", 2), ("grad", 3),
-    ("grad_pair", 3), ("mask", 2), ("mask", 1), ("dec_all", 2),
-    ("mask", 3),
+    ("turn_dec", 0), ("partial", 0), ("turn_dec", 1), ("pair_sum", 0),
+    ("partial", 1), ("pair_sum", 1), ("partial", 2), ("activate", 0),
+    ("pair_sum", 2), ("activate", 1), ("pass_active", 0), ("partial", 3),
+    ("decode", 0), ("activate", 2), ("pass_active", 1), ("pair_sum", 3),
+    ("fold", 0), ("pass_active", 2), ("decode", 1), ("decode", 2),
+    ("activate", 3), ("fold", 1), ("grad", 0), ("fold", 2),
+    ("grad_pair", 0), ("pass_active", 3), ("grad", 1), ("decode", 3),
+    ("grad_pair", 1), ("grad", 2), ("turn_tok", 0), ("mask", 0),
+    ("fold", 3), ("grad_pair", 2), ("grad", 3), ("grad_pair", 3),
+    ("mask", 2), ("mask", 1), ("dec_all", 2), ("keep", 0),
+    ("keep", 1), ("keep", 2), ("mask", 3), ("keep", 3),
 )
 
 
@@ -35,7 +36,7 @@
 
 
 def kernel(chunks, rows, quarter, enc_scale, dec_scale, tok_ref, enc_hbm, dec_hbm, bias_ref, dbias_ref,
-           tok, gp, dec_out, enc_ref, dec_ref, dec_acc, psend, prec, pown, xsend, xrec, act, rpart, rrec, err,
+           tok_t, gp_out, dec_out, tok, gp, enc_ref, dec_ref, dec_flat, dec_acc, psend, prec, pown, xsend, xrec, act, rpart, rrec, err,
            gsend, grec, gown, xgsend, xgrec, loads, sends, recvs):
     layer, feat = lax.axis_index("layer"), lax.axis_index("feat")
     xi, core = layer // 2, layer % 2
@@ -125,13 +126,11 @@
         send(c, CB, other, other, pair_dev)
 
     def decode(c):
-        if c == 0:
-            load_dec.wait()
         arrive(c, CA, act.at[c, (1 - core) * 2 + xi], pair_dev)
         arrive(c, CB, act.at[c, (1 - core) * 2 + (1 - xi)], pair_dev)
-        part = contract_columns(act[c, 0], dec_ref[:, 0:quarter])
+        part = jnp.dot(act[c, 0], dec_flat[0], preferred_element_type=F32)
         for q in range(1, 4):
-            part = part + contract_columns(act[c, q], dec_ref[:, q * quarter:(q + 1) * quarter])
+            part = part + jnp.dot(act[c, q], dec_flat[q], preferred_element_type=F32)
         rpart[c] = (dec_scale * part).astype(BF16).reshape(8, rows, -1)
         for step in (4, 3, 5, 2, 6, 1, 7):
             send(c, RS + step - 1, rpart.at[c, feat_at(step)], rrec.at[c, step - 1], feat_dev(step))
@@ -173,36 +172,55 @@
             gp[c, q] = jnp.where(lit, whole, 0.0).astype(BF16)
             send(c, GM + j, gp.at[c, q], gp.at[c, q], pair_dev)
 
+    def turn_dec(half):
+        if half == 0:
+            load_dec.wait()
+        for q in (2 * half, 2 * half + 1):
+            dec_flat[q] = dec_ref[:, q * quarter:(q + 1) * quarter].T
+
+    def turn_tok(_):
+        tok_t[...] = tok[...].reshape(chunks * 8 * rows, -1).T
+
+    store_gp = [
+        [pltpu.make_async_copy(gp.at[c, pl.ds(h * 2, 2)], gp_out.at[c, pl.ds(h * 2, 2)], loads.at[3 + 2 * c + i])
+         for i, h in enumerate((core, 1 - core))]
+        for c in range(chunks)]
+
+    def keep(c):
+        for j in range(2):
+            arrive(c, GM + j, gp.at[c, (1 - core) * 2 + j], pair_dev)
+        store_gp[c][0].start()
+        store_gp[c][1].start()
+
     store_dec = pltpu.make_async_copy(dec_acc, dec_out, loads.at[2])
 
     def dec_all(_):
-        @pl.loop(0, 4)
-        def _(q):
-            left = err[...].reshape(chunks * 8 * rows, -1)
+        left = err[...].reshape(chunks * 8 * rows, -1).T
+        for q in range(4):
             right = jnp.concatenate([act[c, q] for c in range(chunks)], axis=0)
-            dec_acc[:, columns(q)] = (-LEARN_RATE * dec_scale * contract_rows(left, right)).astype(BF16)
+            step = jnp.dot(left, right, preferred_element_type=F32)
+            dec_acc[:, q * quarter:(q + 1) * quarter] = (-LEARN_RATE * dec_scale * step).astype(BF16)
 
         store_dec.start()
 
     for c in range(chunks):
         gather_begin(c, TOK, tok)
     stages = dict(partial=partial, pair_sum=pair_sum, activate=activate, pass_active=pass_active, decode=decode,
-                  fold=fold, grad=grad, grad_pair=grad_pair, mask=mask, dec_all=dec_all)
+                  fold=fold, grad=grad, grad_pair=grad_pair, mask=mask, dec_all=dec_all,
+                  turn_dec=turn_dec, turn_tok=turn_tok, keep=keep)
     for name, c in ORDER:
         stages[name](c)
     for c in range(chunks):
-        for j in range(2):
-            arrive(c, GM + j, gp.at[c, (1 - core) * 2 + j], pair_dev)
+        for moving in store_gp[c]:
+            moving.wait()
     store_dec.wait()
     for moving in started:
         moving.wait_send()
 
 
 def finish(scale, tok_ref, gp_ref, dec_ref, enc_out, dec_out):
-    chunks = tok_ref.shape[0]
-    left = tok_ref[...].reshape(-1, tok_ref.shape[3])
-    right = jnp.concatenate([gp_ref[c, 0] for c in range(chunks)], axis=0)
-    enc_out[...] = (scale * contract_rows(left, right)).astype(BF16)
+    right = jnp.concatenate([gp_ref[c, 0] for c in range(gp_ref.shape[0])], axis=0)
+    enc_out[...] = (scale * jnp.dot(tok_ref[...], right, preferred_element_type=F32)).astype(BF16)
     dec_out[...] = dec_ref[...]
 
 
@@ -223,20 +241,20 @@
     blocks = pltpu.VMEM((chunks, 8, rows, width), BF16)
     weights = pltpu.VMEM((width, features), BF16)
     step_shape = jax.ShapeDtypeStruct((width, features), BF16)
-    tok, gp, dec_step = pl.pallas_call(
+    tok_t, gp, dec_step = pl.pallas_call(
         functools.partial(kernel, chunks, rows, quarter, enc_scale, dec_scale),
         out_shape=[
-            jax.ShapeDtypeStruct((chunks, 8, rows, width), BF16),
+            jax.ShapeDtypeStruct((width, tokens * 8), BF16),
             jax.ShapeDtypeStruct((chunks, 4, whole, quarter), BF16),
             step_shape,
         ],
         in_specs=[vmem, anywhere, anywhere, vmem, vmem],
-        out_specs=[vmem, vmem, anywhere],
+        out_specs=[vmem, anywhere, anywhere],
         scratch_shapes=[
-            weights, weights, weights, half32, half32, half32, quarter32, quarter32, full16, blocks,
+            blocks, full16, weights, weights, pltpu.VMEM((4, quarter, width), BF16), weights, half32, half32, half32, quarter32, quarter32, full16, blocks,
             pltpu.VMEM((chunks, 7, rows, width), BF16),
             blocks, half16, half16, half32, half16, half16,
-            pltpu.SemaphoreType.DMA((3,)),
+            pltpu.SemaphoreType.DMA((3 + 2 * chunks,)),
             pltpu.SemaphoreType.DMA((chunks, 33)),
             pltpu.SemaphoreType.DMA((chunks, 33)),
         ],
@@ -249,13 +267,13 @@
         out_shape=[step_shape, step_shape],
         grid=(4,),
         in_specs=[
-            pl.BlockSpec((chunks, 8, rows, width), lambda q: (0, 0, 0, 0)),
+            pl.BlockSpec((width, tokens * 8), lambda q: (0, 0)),
             pl.BlockSpec((chunks, 1, whole, quarter), lambda q: (0, q, 0, 0)),
             slab,
         ],
         out_specs=[slab, slab],
         compiler_params=pltpu.CompilerParams(vmem_limit_bytes=60 * 2**20),
-    )(tok, gp, dec_step)
+    )(tok_t, gp, dec_step)
     return enc_step[None], jnp.swapaxes(dec_step, 0, 1)[None]
 
 

time: 91.9 us -> 90.6 us (0.986)
  Pallas kernels: 91.1 us -> 89.7 us
    pallas_call x1, Pallas kernels: 85 us -> 83.8 us  [fused(): pl.pallas_call(functools.partial(kernel, chunks, rows, quarter, enc_scale...]
where the time goes in v3:
time: 90.6 us; the launch traced here: 90.3 us
  Pallas kernels  89.7 us (99%)
    pallas_call x1, Pallas kernels, fused(): pl.pallas_call(functools.partial(kernel, chunks, rows, quarter, enc_scale...  83.8 us
    pallas_call x1, Pallas kernels, fused(): pl.pallas_call(functools.partial(finish, -LEARN_RATE * enc_scale), out_sh...  5.93 us

profile of v3, /device:TPU:0, one launch (start us, length us, event | category | flops | bytes accessed | tf_op | source)
XLA Modules:
  0.0 90.3 jit_solution(8353103979065128431)
XLA Ops:
  0.6 83.8 %shard_map.68 = (bf16[576,512]{1,0:T(8,128)(2,1)}, bf16[4,4,128,512]{3,2,1,0:T(8,128)(2,1)}, bf16[576,2048]{1,0:T(8,128)(2,1)}) custom-call(bf16[64,576]{1,0:T(8,128)(2,1)} %bitcast.12, bf16[576,2048]{1,0:T(8,128)(2,1)} %bitcast.10, bf16[576,2048]{1,0:T(8,128)(2,1)} %bitcast.11, f32[4,1,512]{2,1,0:T(1,128)} %bitcast.13, f32[1,576]{1,0:T(1,128)} %dbias_ref.1), custom_call_target="tpu_custom_call" | custom-call | tf_op jit(solution)/shard_map/pallas_call | solution.py:244
  84.4 5.9 %shard_map.69 = (bf16[576,2048]{1,0:T(8,128)(2,1)}, bf16[576,2048]{1,0:T(8,128)(2,1)}) custom-call(bf16[576,512]{1,0:T(8,128)(2,1)} %get-tuple-element.7.tok_ref, bf16[4,4,128,512]{3,2,1,0:T(8,128)(2,1)} %get-tuple-element.8.gp_ref, bf16[576,2048]{1,0:T(8,128)(2,1)} %get-tuple-element.9.dec_ref), custom_call_target="tpu_custom_call" | custom-call | tf_op jit(solution)/shard_map/pallas_call | solution.py:265

commit v4 on v3

--- a/solution.py
+++ b/solution.py
@@ -36,7 +36,7 @@
 
 
 def kernel(chunks, rows, quarter, enc_scale, dec_scale, tok_ref, enc_hbm, dec_hbm, bias_ref, dbias_ref,
-           tok_t, gp_out, dec_out, tok, gp, enc_ref, dec_ref, dec_flat, dec_acc, psend, prec, pown, xsend, xrec, act, rpart, rrec, err,
+           tok_t, gp, dec_acc, tok, enc_ref, dec_ref, dec_flat, psend, prec, pown, xsend, xrec, act, rpart, rrec, err,
            gsend, grec, gown, xgsend, xgrec, loads, sends, recvs):
     layer, feat = lax.axis_index("layer"), lax.axis_index("feat")
     xi, core = layer // 2, layer % 2
@@ -181,18 +181,9 @@
     def turn_tok(_):
         tok_t[...] = tok[...].reshape(chunks * 8 * rows, -1).T
 
-    store_gp = [
-        [pltpu.make_async_copy(gp.at[c, pl.ds(h * 2, 2)], gp_out.at[c, pl.ds(h * 2, 2)], loads.at[3 + 2 * c + i])
-         for i, h in enumerate((core, 1 - core))]
-        for c in range(chunks)]
-
     def keep(c):
         for j in range(2):
             arrive(c, GM + j, gp.at[c, (1 - core) * 2 + j], pair_dev)
-        store_gp[c][0].start()
-        store_gp[c][1].start()
-
-    store_dec = pltpu.make_async_copy(dec_acc, dec_out, loads.at[2])
 
     def dec_all(_):
         left = err[...].reshape(chunks * 8 * rows, -1).T
@@ -200,8 +191,6 @@
             right = jnp.concatenate([act[c, q] for c in range(chunks)], axis=0)
             step = jnp.dot(left, right, preferred_element_type=F32)
             dec_acc[:, q * quarter:(q + 1) * quarter] = (-LEARN_RATE * dec_scale * step).astype(BF16)
-
-        store_dec.start()
 
     for c in range(chunks):
         gather_begin(c, TOK, tok)
@@ -210,18 +199,23 @@
                   turn_dec=turn_dec, turn_tok=turn_tok, keep=keep)
     for name, c in ORDER:
         stages[name](c)
-    for c in range(chunks):
-        for moving in store_gp[c]:
-            moving.wait()
-    store_dec.wait()
     for moving in started:
         moving.wait_send()
 
 
-def finish(scale, tok_ref, gp_ref, dec_ref, enc_out, dec_out):
-    right = jnp.concatenate([gp_ref[c, 0] for c in range(gp_ref.shape[0])], axis=0)
-    enc_out[...] = (scale * jnp.dot(tok_ref[...], right, preferred_element_type=F32)).astype(BF16)
-    dec_out[...] = dec_ref[...]
+def finish(scale, tok_ref, gp_ref, dec_ref, enc_out, dec_out, slabs, sems):
+    store_dec = pltpu.make_async_copy(dec_ref, dec_out, sems.at[0])
+    store_dec.start()
+    quarter = gp_ref.shape[3]
+    stores = []
+    for q in range(4):
+        right = jnp.concatenate([gp_ref[c, q] for c in range(gp_ref.shape[0])], axis=0)
+        slabs[q] = (scale * jnp.dot(tok_ref[...], right, preferred_element_type=F32)).astype(BF16)
+        store = pltpu.make_async_copy(slabs.at[q], enc_out.at[:, q * quarter:(q + 1) * quarter], sems.at[1 + q])
+        store.start()
+        stores.append(store)
+    for store in [store_dec] + stores:
+        store.wait()
 
 
 def fused(layer_acts, enc_weight, dec_weight, enc_bias, dec_bias):
@@ -244,35 +238,30 @@
     tok_t, gp, dec_step = pl.pallas_call(
         functools.partial(kernel, chunks, rows, quarter, enc_scale, dec_scale),
         out_shape=[
-            jax.ShapeDtypeStruct((width, tokens * 8), BF16),
-            jax.ShapeDtypeStruct((chunks, 4, whole, quarter), BF16),
-            step_shape,
+            pltpu.VMEM((width, tokens * 8), BF16),
+            full16,
+            weights,
         ],
         in_specs=[vmem, anywhere, anywhere, vmem, vmem],
-        out_specs=[vmem, anywhere, anywhere],
+        out_specs=[vmem] * 3,
         scratch_shapes=[
-            blocks, full16, weights, weights, pltpu.VMEM((4, quarter, width), BF16), weights, half32, half32, half32, quarter32, quarter32, full16, blocks,
+            blocks, weights, weights, pltpu.VMEM((4, quarter, width), BF16), half32, half32, half32, quarter32, quarter32, full16, blocks,
             pltpu.VMEM((chunks, 7, rows, width), BF16),
             blocks, half16, half16, half32, half16, half16,
-            pltpu.SemaphoreType.DMA((3 + 2 * chunks,)),
+            pltpu.SemaphoreType.DMA((2,)),
             pltpu.SemaphoreType.DMA((chunks, 33)),
             pltpu.SemaphoreType.DMA((chunks, 33)),
         ],
         compiler_params=pltpu.CompilerParams(
             collective_id=0, has_side_effects=True, vmem_limit_bytes=56 * 2**20),
     )(layer_acts[0], enc_weight[0], jnp.swapaxes(dec_weight[0], 0, 1), enc_bias.reshape(4, 1, quarter), dec_bias)
-    slab = pl.BlockSpec((width, quarter), lambda q: (0, q))
     enc_step, dec_step = pl.pallas_call(
         functools.partial(finish, -LEARN_RATE * enc_scale),
         out_shape=[step_shape, step_shape],
-        grid=(4,),
-        in_specs=[
-            pl.BlockSpec((width, tokens * 8), lambda q: (0, 0)),
-            pl.BlockSpec((chunks, 1, whole, quarter), lambda q: (0, q, 0, 0)),
-            slab,
-        ],
-        out_specs=[slab, slab],
-        compiler_params=pltpu.CompilerParams(vmem_limit_bytes=60 * 2**20),
+        in_specs=[vmem] * 3,
+        out_specs=[anywhere] * 2,
+        scratch_shapes=[pltpu.VMEM((4, width, quarter), BF16), pltpu.SemaphoreType.DMA((5,))],
+        compiler_params=pltpu.CompilerParams(vmem_limit_bytes=16 * 2**20),
     )(tok_t, gp, dec_step)
     return enc_step[None], jnp.swapaxes(dec_step, 0, 1)[None]
 

time: 90.6 us -> 85.1 us (0.939)
  Pallas kernels: 89.7 us -> 84.3 us
    pallas_call x1, Pallas kernels: 5.93 us -> 2.25 us  [fused(): pl.pallas_call(functools.partial(finish, -LEARN_RATE * enc_scale), out_sh...]
    pallas_call x1, Pallas kernels: 83.8 us -> 82.1 us  [fused(): pl.pallas_call(functools.partial(kernel, chunks, rows, quarter, enc_scale...]
where the time goes in v4:
time: 85.1 us; the launch traced here: 85 us
  Pallas kernels  84.3 us (99%)
    pallas_call x1, Pallas kernels, fused(): pl.pallas_call(functools.partial(kernel, chunks, rows, quarter, enc_scale...  82.1 us
    pallas_call x1, Pallas kernels, fused(): pl.pallas_call(functools.partial(finish, -LEARN_RATE * enc_scale), out_sh...  2.25 us

profile of v4, /device:TPU:0, one launch (start us, length us, event | category | flops | bytes accessed | tf_op | source)
XLA Modules:
  0.0 85.0 jit_solution(14335476473025803036)
XLA Ops:
  0.6 82.1 %shard_map.68 = (bf16[576,512]{1,0:T(8,128)(2,1)S(1)}, bf16[4,4,128,512]{3,2,1,0:T(8,128)(2,1)S(1)}, bf16[576,2048]{1,0:T(8,128)(2,1)S(1)}) custom-call(bf16[64,576]{1,0:T(8,128)(2,1)} %bitcast.12, bf16[576,2048]{1,0:T(8,128)(2,1)} %bitcast.10, bf16[576,2048]{1,0:T(8,128)(2,1)} %bitcast.11, f32[4,1,512]{2,1,0:T(1,128)} %bitcast.13, f32[1,576]{1,0:T(1,128)} %dbias_ref.1), custom_call_target="tpu_custom_call" | custom-call | tf_op jit(solution)/shard_map/pallas_call | solution.py:238
  82.7 2.3 %shard_map.69 = (bf16[576,2048]{1,0:T(8,128)(2,1)}, bf16[576,2048]{1,0:T(8,128)(2,1)}) custom-call(bf16[576,512]{1,0:T(8,128)(2,1)S(1)} %get-tuple-element.7.tok_ref, bf16[4,4,128,512]{3,2,1,0:T(8,128)(2,1)S(1)} %get-tuple-element.8.gp_ref, bf16[576,2048]{1,0:T(8,128)(2,1)S(1)} %get-tuple-element.9.dec_ref), custom_call_target="tpu_custom_call" | custom-call | tf_op jit(solution)/shard_map/pallas_call | solution.py:258

commit v5 on v4

--- a/solution.py
+++ b/solution.py
@@ -14,16 +14,17 @@
 
 ORDER = (
     ("turn_dec", 0), ("partial", 0), ("turn_dec", 1), ("pair_sum", 0),
-    ("partial", 1), ("pair_sum", 1), ("partial", 2), ("activate", 0),
-    ("pair_sum", 2), ("activate", 1), ("pass_active", 0), ("partial", 3),
-    ("decode", 0), ("activate", 2), ("pass_active", 1), ("pair_sum", 3),
-    ("fold", 0), ("pass_active", 2), ("decode", 1), ("decode", 2),
-    ("activate", 3), ("fold", 1), ("grad", 0), ("fold", 2),
-    ("grad_pair", 0), ("pass_active", 3), ("grad", 1), ("decode", 3),
-    ("grad_pair", 1), ("grad", 2), ("turn_tok", 0), ("mask", 0),
-    ("fold", 3), ("grad_pair", 2), ("grad", 3), ("grad_pair", 3),
-    ("mask", 2), ("mask", 1), ("dec_all", 2), ("keep", 0),
-    ("keep", 1), ("keep", 2), ("mask", 3), ("keep", 3),
+    ("partial", 1), ("rest", 0), ("pair_sum", 1), ("rest", 1),
+    ("activate", 0), ("partial", 2), ("activate", 1), ("pair_sum", 2),
+    ("rest", 2), ("pass_active", 0), ("partial", 3), ("pass_active", 1),
+    ("decode", 0), ("pair_sum", 3), ("decode", 1), ("rest", 3),
+    ("fold", 0), ("activate", 3), ("activate", 2), ("pass_active", 3),
+    ("fold", 1), ("grad", 0), ("pass_active", 2), ("decode", 3),
+    ("decode", 2), ("grad_pair", 0), ("grad", 1), ("fold", 3),
+    ("grad_pair", 1), ("fold", 2), ("grad", 3), ("grad_pair", 3),
+    ("grad", 2), ("grad_pair", 2), ("turn_tok", 0), ("mask", 0),
+    ("mask", 3), ("mask", 1), ("dec_all", 0), ("keep", 0),
+    ("keep", 1), ("keep", 3), ("mask", 2), ("keep", 2),
 )
 
 
@@ -36,13 +37,14 @@
 
 
 def kernel(chunks, rows, quarter, enc_scale, dec_scale, tok_ref, enc_hbm, dec_hbm, bias_ref, dbias_ref,
-           tok_t, gp, dec_acc, tok, enc_ref, dec_ref, dec_flat, psend, prec, pown, xsend, xrec, act, rpart, rrec, err,
+           tok_t, gp, dec_acc, tok, tok_x, enc_ref, enc_x, dec_ref, dec_flat, psend, prec, pown, bsend, brec, bown, xsend, xrec, act, rpart, rrec, err,
            gsend, grec, gown, xgsend, xgrec, loads, sends, recvs):
     layer, feat = lax.axis_index("layer"), lax.axis_index("feat")
     xi, core = layer // 2, layer % 2
     pair_dev = (xi * 2 + (1 - core), feat)
     x_dev = ((1 - xi) * 2 + core, feat)
     steps = range(1, 8)
+    ship = enc_x.shape[2]
 
     load_enc = pltpu.make_async_copy(enc_hbm, enc_ref, loads.at[0])
     load_dec = pltpu.make_async_copy(dec_hbm, dec_ref, loads.at[1])
@@ -87,36 +89,48 @@
         for step in steps:
             arrive(c, base + step - 1, buf.at[c, feat_at(-step)], feat_dev(-step))
 
-    TOK, ERR, RS, PAIR, XP, XA, CA, CB, GP, GX, GM = 0, 7, 14, 21, 23, 24, 25, 26, 27, 29, 31
-
-    def columns(q):
-        return pl.ds(pl.multiple_of(q * quarter, quarter), quarter)
-
-    halves = ((0, 1 - xi), (1, xi))
+    TOK, ERR, RS, PAIR, XP, XA, CA, CB, GP, GX, GM, TX, TOK_X, WX = 0, 7, 14, 21, 23, 24, 25, 26, 27, 29, 31, 33, 34, 41
+
+    def columns(q, skip=0):
+        return pl.ds(pl.multiple_of(q * quarter + skip, 128), quarter - skip)
 
     def partial(c):
         gather_end(c, TOK, tok)
         if c == 0:
             load_enc.wait()
         x = tok[c].reshape(8 * rows, -1)
-        for i, j in halves:
-            psend[c, i] = jnp.dot(x, enc_ref[:, columns((1 - core) * 2 + j)], preferred_element_type=F32)
-            send(c, PAIR + i, psend.at[c, i], prec.at[c, i], pair_dev)
-        for i, j in halves:
-            pown[c, i] = jnp.dot(x, enc_ref[:, columns(core * 2 + j)], preferred_element_type=F32)
+        psend[c] = jnp.dot(x, enc_ref[:, columns((1 - core) * 2 + 1 - xi, ship)], preferred_element_type=F32)
+        send(c, PAIR, psend.at[c], prec.at[c], pair_dev)
+        pown[c] = jnp.dot(x, enc_ref[:, columns(core * 2 + 1 - xi, ship)], preferred_element_type=F32)
 
     def pair_sum(c):
-        arrive(c, PAIR, prec.at[c, 0], pair_dev)
-        xsend[c] = pown[c, 0] + prec[c, 0]
+        arrive(c, PAIR, prec.at[c], pair_dev)
+        xsend[c] = pown[c] + prec[c]
         send(c, XP, xsend.at[c], xrec.at[c], x_dev)
 
+    def rest(c):
+        gather_end(c, TOK_X, tok_x)
+        if c == 0:
+            for h in range(2):
+                arrive(0, WX + h, enc_x.at[h], x_dev)
+        x = tok[c].reshape(8 * rows, -1)
+        x_far = tok_x[c].reshape(8 * rows, -1)
+        for h, dst in ((1 - core, bsend), (core, bown)):
+            dst[c] = jnp.dot(x, enc_ref[:, columns(h * 2 + xi)], preferred_element_type=F32)
+            dst[c, :, 0:ship] += jnp.dot(x_far, enc_x[h], preferred_element_type=F32)
+            if dst is bsend:
+                send(c, PAIR + 1, bsend.at[c], brec.at[c], pair_dev)
+
     def activate(c):
-        arrive(c, PAIR + 1, prec.at[c, 1], pair_dev)
+        arrive(c, PAIR + 1, brec.at[c], pair_dev)
+        mine = core * 2 + xi
+        bias = bias_ref[mine]
+        near = bown[c] + brec[c]
         arrive(c, XP, xrec.at[c], x_dev)
-        total = pown[c, 1] + prec[c, 1] + xrec[c]
-        mine = core * 2 + xi
-        preact = enc_scale * total + bias_ref[mine]
-        act[c, mine] = jnp.maximum(preact, 0.0).astype(BF16)
+        first = enc_scale * near[:, 0:ship] + bias[:, 0:ship]
+        second = enc_scale * (near[:, ship:] + xrec[c]) + bias[:, ship:]
+        act[c, mine, :, 0:ship] = jnp.maximum(first, 0.0).astype(BF16)
+        act[c, mine, :, ship:quarter] = jnp.maximum(second, 0.0).astype(BF16)
         send(c, XA, act.at[c, mine], act.at[c, mine], x_dev)
         send(c, CA, act.at[c, mine], act.at[c, mine], pair_dev)
 
@@ -192,10 +206,25 @@
             step = jnp.dot(left, right, preferred_element_type=F32)
             dec_acc[:, q * quarter:(q + 1) * quarter] = (-LEARN_RATE * dec_scale * step).astype(BF16)
 
+    def spread(c):
+        arrive(c, TX, tok_x.at[c, feat], x_dev)
+        gather_begin(c, TOK_X, tok_x)
+
+    gather_begin(0, TOK, tok)
     for c in range(chunks):
+        own = tok.at[c, feat]
+        send(c, TX, own, tok_x.at[c, feat], x_dev)
+    for h in range(2):
+        sent = pl.ds(pl.multiple_of((h * 2 + 1 - xi) * quarter, quarter), ship)
+        send(0, WX + h, enc_hbm.at[:, sent], enc_x.at[h], x_dev)
+    gather_begin(1, TOK, tok)
+    spread(0)
+    spread(1)
+    for c in range(2, chunks):
         gather_begin(c, TOK, tok)
+        spread(c)
     stages = dict(partial=partial, pair_sum=pair_sum, activate=activate, pass_active=pass_active, decode=decode,
-                  fold=fold, grad=grad, grad_pair=grad_pair, mask=mask, dec_all=dec_all,
+                  fold=fold, grad=grad, grad_pair=grad_pair, mask=mask, dec_all=dec_all, rest=rest,
                   turn_dec=turn_dec, turn_tok=turn_tok, keep=keep)
     for name, c in ORDER:
         stages[name](c)
@@ -230,7 +259,9 @@
     anywhere = pl.BlockSpec(memory_space=pl.ANY)
     half32 = pltpu.VMEM((chunks, 2, whole, quarter), F32)
     half16 = pltpu.VMEM((chunks, 2, whole, quarter), BF16)
+    ship = quarter // 4
     quarter32 = pltpu.VMEM((chunks, whole, quarter), F32)
+    short32 = pltpu.VMEM((chunks, whole, quarter - ship), F32)
     full16 = pltpu.VMEM((chunks, 4, whole, quarter), BF16)
     blocks = pltpu.VMEM((chunks, 8, rows, width), BF16)
     weights = pltpu.VMEM((width, features), BF16)
@@ -245,12 +276,14 @@
         in_specs=[vmem, anywhere, anywhere, vmem, vmem],
         out_specs=[vmem] * 3,
         scratch_shapes=[
-            blocks, weights, weights, pltpu.VMEM((4, quarter, width), BF16), half32, half32, half32, quarter32, quarter32, full16, blocks,
+            blocks, blocks, weights, pltpu.VMEM((2, width, ship), BF16), weights,
+            pltpu.VMEM((4, quarter, width), BF16), short32, short32, short32, quarter32, quarter32, quarter32,
+            short32, short32, full16, blocks,
             pltpu.VMEM((chunks, 7, rows, width), BF16),
             blocks, half16, half16, half32, half16, half16,
             pltpu.SemaphoreType.DMA((2,)),
-            pltpu.SemaphoreType.DMA((chunks, 33)),
-            pltpu.SemaphoreType.DMA((chunks, 33)),
+            pltpu.SemaphoreType.DMA((chunks, 43)),
+            pltpu.SemaphoreType.DMA((chunks, 43)),
         ],
         compiler_params=pltpu.CompilerParams(
             collective_id=0, has_side_effects=True, vmem_limit_bytes=56 * 2**20),

time: 85.1 us -> 89.5 us (1.052)
  Pallas kernels: 84.3 us -> 88.7 us
    pallas_call x1, Pallas kernels: 82.1 us -> 86.5 us  [fused(): pl.pallas_call(functools.partial(kernel, chunks, rows, quarter, enc_scale...]
where the time goes in v5:
time: 89.5 us; the launch traced here: 89.4 us
  Pallas kernels  88.7 us (99%)
    pallas_call x1, Pallas kernels, fused(): pl.pallas_call(functools.partial(kernel, chunks, rows, quarter, enc_scale...  86.5 us
    pallas_call x1, Pallas kernels, fused(): pl.pallas_call(functools.partial(finish, -LEARN_RATE * enc_scale), out_sh...  2.25 us

profile of v5, /device:TPU:0, one launch (start us, length us, event | category | flops | bytes accessed | tf_op | source)
XLA Modules:
  0.0 89.4 jit_solution(15844801315655881945)
XLA Ops:
  0.6 86.5 %shard_map.68 = (bf16[576,512]{1,0:T(8,128)(2,1)S(1)}, bf16[4,4,128,512]{3,2,1,0:T(8,128)(2,1)S(1)}, bf16[576,2048]{1,0:T(8,128)(2,1)S(1)}) custom-call(bf16[64,576]{1,0:T(8,128)(2,1)} %bitcast.12, bf16[576,2048]{1,0:T(8,128)(2,1)} %bitcast.10, bf16[576,2048]{1,0:T(8,128)(2,1)} %bitcast.11, f32[4,1,512]{2,1,0:T(1,128)} %bitcast.13, f32[1,576]{1,0:T(1,128)} %dbias_ref.1), custom_call_target="tpu_custom_call" | custom-call | tf_op jit(solution)/shard_map/pallas_call | solution.py:269
  87.1 2.3 %shard_map.69 = (bf16[576,2048]{1,0:T(8,128)(2,1)}, bf16[576,2048]{1,0:T(8,128)(2,1)}) custom-call(bf16[576,512]{1,0:T(8,128)(2,1)S(1)} %get-tuple-element.7.tok_ref, bf16[4,4,128,512]{3,2,1,0:T(8,128)(2,1)S(1)} %get-tuple-element.8.gp_ref, bf16[576,2048]{1,0:T(8,128)(2,1)S(1)} %get-tuple-element.9.dec_ref), custom_call_target="tpu_custom_call" | custom-call | tf_op jit(solution)/shard_map/pallas_call | solution.py:291

commit v6 on v4

--- a/solution.py
+++ b/solution.py
@@ -14,15 +14,16 @@
 
 ORDER = (
     ("turn_dec", 0), ("partial", 0), ("turn_dec", 1), ("pair_sum", 0),
-    ("partial", 1), ("pair_sum", 1), ("partial", 2), ("activate", 0),
-    ("pair_sum", 2), ("activate", 1), ("pass_active", 0), ("partial", 3),
+    ("partial", 1), ("pair_sum", 1), ("activate", 0), ("partial", 2),
+    ("pair_sum", 2), ("partial", 3), ("pass_active", 0), ("activate", 1),
     ("decode", 0), ("activate", 2), ("pass_active", 1), ("pair_sum", 3),
-    ("fold", 0), ("pass_active", 2), ("decode", 1), ("decode", 2),
-    ("activate", 3), ("fold", 1), ("grad", 0), ("fold", 2),
-    ("grad_pair", 0), ("pass_active", 3), ("grad", 1), ("decode", 3),
-    ("grad_pair", 1), ("grad", 2), ("turn_tok", 0), ("mask", 0),
-    ("fold", 3), ("grad_pair", 2), ("grad", 3), ("grad_pair", 3),
-    ("mask", 2), ("mask", 1), ("dec_all", 2), ("keep", 0),
+    ("fold", 0), ("decode", 1), ("pass_active", 2), ("pass_error", 0),
+    ("decode", 2), ("activate", 3), ("fold", 1), ("grad", 0),
+    ("grad_pair", 0), ("fold", 2), ("pass_active", 3), ("pass_error", 1),
+    ("decode", 3), ("grad", 1), ("pass_error", 2), ("grad_pair", 1),
+    ("fold", 3), ("grad", 2), ("pass_error", 3), ("grad_pair", 2),
+    ("grad", 3), ("mask", 1), ("grad_pair", 3), ("turn_tok", 0),
+    ("mask", 0), ("mask", 2), ("dec_all", 0), ("keep", 0),
     ("keep", 1), ("keep", 2), ("mask", 3), ("keep", 3),
 )
 
@@ -43,6 +44,8 @@
     pair_dev = (xi * 2 + (1 - core), feat)
     x_dev = ((1 - xi) * 2 + core, feat)
     steps = range(1, 8)
+    y_feat = (feat // 2) * 2 + (1 - feat % 2)
+    y_dev = (layer, y_feat)
 
     load_enc = pltpu.make_async_copy(enc_hbm, enc_ref, loads.at[0])
     load_dec = pltpu.make_async_copy(dec_hbm, dec_ref, loads.at[1])
@@ -86,6 +89,26 @@
     def gather_end(c, base, buf):
         for step in steps:
             arrive(c, base + step - 1, buf.at[c, feat_at(-step)], feat_dev(-step))
+
+    def staged_begin(c, base, buf):
+        own = buf.at[c, feat]
+        for step in (4, 2, 6):
+            send(c, base + step - 1, own, own, feat_dev(step))
+        send(c, base, own, own, y_dev)
+
+    def staged_pass(c, base, buf):
+        for step in (2, 6, 4):
+            slot = buf.at[c, feat_at(-step)]
+            arrive(c, base + step - 1, slot, feat_dev(-step))
+            send(c, base + step, slot, slot, y_dev)
+
+    def staged_end(c, base, buf):
+        arrive(c, base, buf.at[c, y_feat], y_dev)
+        for step in (2, 6, 4):
+            arrive(c, base + step, buf.at[c, lax.rem(y_feat - step + 8, 8)], y_dev)
+
+    def pass_error(c):
+        staged_pass(c, ERR, err)
 
     TOK, ERR, RS, PAIR, XP, XA, CA, CB, GP, GX, GM = 0, 7, 14, 21, 23, 24, 25, 26, 27, 29, 31
 
@@ -142,10 +165,10 @@
             recon = recon + rrec[c, step - 1].astype(F32)
         own = tok_ref[c * rows:(c + 1) * rows, :].astype(F32)
         err[c, feat] = (recon + dbias_ref[...] - own).astype(BF16)
-        gather_begin(c, ERR, err)
+        staged_begin(c, ERR, err)
 
     def grad(c):
-        gather_end(c, ERR, err)
+        staged_end(c, ERR, err)
         e = err[c].reshape(8 * rows, -1)
         for j in range(2):
             g = jnp.dot(e, dec_ref[:, columns((1 - core) * 2 + j)], preferred_element_type=F32)
@@ -195,7 +218,7 @@
     for c in range(chunks):
         gather_begin(c, TOK, tok)
     stages = dict(partial=partial, pair_sum=pair_sum, activate=activate, pass_active=pass_active, decode=decode,
-                  fold=fold, grad=grad, grad_pair=grad_pair, mask=mask, dec_all=dec_all,
+                  fold=fold, grad=grad, grad_pair=grad_pair, mask=mask, dec_all=dec_all, pass_error=pass_error,
                   turn_dec=turn_dec, turn_tok=turn_tok, keep=keep)
     for name, c in ORDER:
         stages[name](c)

time: 85.1 us -> 83.5 us (0.981)
  Pallas kernels: 84.3 us -> 82.6 us
    pallas_call x1, Pallas kernels: 82.1 us -> 80.3 us  [fused(): pl.pallas_call(functools.partial(kernel, chunks, rows, quarter, enc_scale...]
where the time goes in v6:
time: 83.5 us; the launch traced here: 83.2 us
  Pallas kernels  82.6 us (99%)
    pallas_call x1, Pallas kernels, fused(): pl.pallas_call(functools.partial(kernel, chunks, rows, quarter, enc_scale...  80.3 us
    pallas_call x1, Pallas kernels, fused(): pl.pallas_call(functools.partial(finish, -LEARN_RATE * enc_scale), out_sh...  2.25 us

profile of v6, /device:TPU:0, one launch (start us, length us, event | category | flops | bytes accessed | tf_op | source)
XLA Modules:
  0.0 83.2 jit_solution(10381384229055204089)
XLA Ops:
  0.6 80.3 %shard_map.68 = (bf16[576,512]{1,0:T(8,128)(2,1)S(1)}, bf16[4,4,128,512]{3,2,1,0:T(8,128)(2,1)S(1)}, bf16[576,2048]{1,0:T(8,128)(2,1)S(1)}) custom-call(bf16[64,576]{1,0:T(8,128)(2,1)} %bitcast.12, bf16[576,2048]{1,0:T(8,128)(2,1)} %bitcast.10, bf16[576,2048]{1,0:T(8,128)(2,1)} %bitcast.11, f32[4,1,512]{2,1,0:T(1,128)} %bitcast.13, f32[1,576]{1,0:T(1,128)} %dbias_ref.1), custom_call_target="tpu_custom_call" | custom-call | tf_op jit(solution)/shard_map/pallas_call | solution.py:261
  80.9 2.3 %shard_map.69 = (bf16[576,2048]{1,0:T(8,128)(2,1)}, bf16[576,2048]{1,0:T(8,128)(2,1)}) custom-call(bf16[576,512]{1,0:T(8,128)(2,1)S(1)} %get-tuple-element.7.tok_ref, bf16[4,4,128,512]{3,2,1,0:T(8,128)(2,1)S(1)} %get-tuple-element.8.gp_ref, bf16[576,2048]{1,0:T(8,128)(2,1)S(1)} %get-tuple-element.9.dec_ref), custom_call_target="tpu_custom_call" | custom-call | tf_op jit(solution)/shard_map/pallas_call | solution.py:281

commit v7 on v6

--- a/solution.py
+++ b/solution.py
@@ -13,18 +13,19 @@
 BF16 = jnp.bfloat16
 
 ORDER = (
-    ("turn_dec", 0), ("partial", 0), ("turn_dec", 1), ("pair_sum", 0),
-    ("partial", 1), ("pair_sum", 1), ("activate", 0), ("partial", 2),
-    ("pair_sum", 2), ("partial", 3), ("pass_active", 0), ("activate", 1),
-    ("decode", 0), ("activate", 2), ("pass_active", 1), ("pair_sum", 3),
-    ("fold", 0), ("decode", 1), ("pass_active", 2), ("pass_error", 0),
-    ("decode", 2), ("activate", 3), ("fold", 1), ("grad", 0),
-    ("grad_pair", 0), ("fold", 2), ("pass_active", 3), ("pass_error", 1),
-    ("decode", 3), ("grad", 1), ("pass_error", 2), ("grad_pair", 1),
-    ("fold", 3), ("grad", 2), ("pass_error", 3), ("grad_pair", 2),
-    ("grad", 3), ("mask", 1), ("grad_pair", 3), ("turn_tok", 0),
-    ("mask", 0), ("mask", 2), ("dec_all", 0), ("keep", 0),
-    ("keep", 1), ("keep", 2), ("mask", 3), ("keep", 3),
+    ("turn_dec", 0), ("partial", 0), ("pass_tok", 1), ("turn_dec", 1),
+    ("pair_sum", 0), ("pass_tok", 2), ("partial", 1), ("pass_tok", 3),
+    ("pair_sum", 1), ("activate", 0), ("partial", 2), ("pair_sum", 2),
+    ("partial", 3), ("pass_active", 0), ("activate", 1), ("decode", 0),
+    ("activate", 2), ("pass_active", 1), ("pair_sum", 3), ("fold", 0),
+    ("decode", 1), ("pass_active", 2), ("pass_error", 0), ("decode", 2),
+    ("activate", 3), ("fold", 1), ("grad", 0), ("grad_pair", 0),
+    ("fold", 2), ("pass_active", 3), ("pass_error", 1), ("decode", 3),
+    ("grad", 1), ("pass_error", 2), ("grad_pair", 1), ("fold", 3),
+    ("grad", 2), ("pass_error", 3), ("grad_pair", 2), ("grad", 3),
+    ("mask", 1), ("grad_pair", 3), ("turn_tok", 0), ("mask", 0),
+    ("mask", 2), ("dec_all", 0), ("keep", 0), ("keep", 1),
+    ("keep", 2), ("mask", 3), ("keep", 3),
 )
 
 
@@ -107,6 +108,9 @@
         for step in (2, 6, 4):
             arrive(c, base + step, buf.at[c, lax.rem(y_feat - step + 8, 8)], y_dev)
 
+    def pass_tok(c):
+        staged_pass(c, TOK, tok)
+
     def pass_error(c):
         staged_pass(c, ERR, err)
 
@@ -118,7 +122,10 @@
     halves = ((0, 1 - xi), (1, xi))
 
     def partial(c):
-        gather_end(c, TOK, tok)
+        if c == 0:
+            gather_end(c, TOK, tok)
+        else:
+            staged_end(c, TOK, tok)
         if c == 0:
             load_enc.wait()
         x = tok[c].reshape(8 * rows, -1)
@@ -215,10 +222,11 @@
             step = jnp.dot(left, right, preferred_element_type=F32)
             dec_acc[:, q * quarter:(q + 1) * quarter] = (-LEARN_RATE * dec_scale * step).astype(BF16)
 
-    for c in range(chunks):
-        gather_begin(c, TOK, tok)
+    gather_begin(0, TOK, tok)
+    for c in range(1, chunks):
+        staged_begin(c, TOK, tok)
     stages = dict(partial=partial, pair_sum=pair_sum, activate=activate, pass_active=pass_active, decode=decode,
-                  fold=fold, grad=grad, grad_pair=grad_pair, mask=mask, dec_all=dec_all, pass_error=pass_error,
+                  fold=fold, grad=grad, grad_pair=grad_pair, mask=mask, dec_all=dec_all, pass_error=pass_error, pass_tok=pass_tok,
                   turn_dec=turn_dec, turn_tok=turn_tok, keep=keep)
     for name, c in ORDER:
         stages[name](c)

time: 83.5 us -> 83.4 us (level)
  no operation moved by 1% of the time
where the time goes in v7:
time: 83.4 us; the launch traced here: 83.1 us
  Pallas kernels  82.5 us (99%)
    pallas_call x1, Pallas kernels, fused(): pl.pallas_call(functools.partial(kernel, chunks, rows, quarter, enc_scale...  80.2 us
    pallas_call x1, Pallas kernels, fused(): pl.pallas_call(functools.partial(finish, -LEARN_RATE * enc_scale), out_sh...  2.25 us

profile of v7, /device:TPU:0, one launch (start us, length us, event | category | flops | bytes accessed | tf_op | source)
XLA Modules:
  0.0 83.1 jit_solution(4587433235060782073)
XLA Ops:
  0.6 80.2 %shard_map.68 = (bf16[576,512]{1,0:T(8,128)(2,1)S(1)}, bf16[4,4,128,512]{3,2,1,0:T(8,128)(2,1)S(1)}, bf16[576,2048]{1,0:T(8,128)(2,1)S(1)}) custom-call(bf16[64,576]{1,0:T(8,128)(2,1)} %bitcast.12, bf16[576,2048]{1,0:T(8,128)(2,1)} %bitcast.10, bf16[576,2048]{1,0:T(8,128)(2,1)} %bitcast.11, f32[4,1,512]{2,1,0:T(1,128)} %bitcast.13, f32[1,576]{1,0:T(1,128)} %dbias_ref.1), custom_call_target="tpu_custom_call" | custom-call | tf_op jit(solution)/shard_map/pallas_call | solution.py:269
  80.9 2.3 %shard_map.69 = (bf16[576,2048]{1,0:T(8,128)(2,1)}, bf16[576,2048]{1,0:T(8,128)(2,1)}) custom-call(bf16[576,512]{1,0:T(8,128)(2,1)S(1)} %get-tuple-element.7.tok_ref, bf16[4,4,128,512]{3,2,1,0:T(8,128)(2,1)S(1)} %get-tuple-element.8.gp_ref, bf16[576,2048]{1,0:T(8,128)(2,1)S(1)} %get-tuple-element.9.dec_ref), custom_call_target="tpu_custom_call" | custom-call | tf_op jit(solution)/shard_map/pallas_call | solution.py:289
